TPU v7x, 256 devices: a whole 4x4x8 slice. The times are simulated.
256 devices in a mesh: node: 32 (over y, z), col: 8 (over x, core).
Axes of the slice: x: 4, y: 4, z: 8, core: 2. Of those that a mesh axis runs over, the one named last changes fastest.
Arguments:
- tile_values: bfloat16 [12288, 128, 128], P('node'), as said below
- tile_rows: int32 [12288], P('node'), may hold values from 0 to 3, as said below
- tile_cols: int32 [12288], P('node'), may hold values from 0 to 127, as said below
- tile_live: int32 [32], P('node'), may hold values from 192 to 384
- degrees: int32 [16384], P('node'), may hold values from 0 to 4095
- projection: int32 [16384, 512], P('node', 'col'), may hold values from -1 to 1
- term_weights: float32 [4], replicated, may hold values from 0.25 to 1.5
Outputs:
- embedding: float32 [16384, 512], P('node', 'col')
Inputs may be any that keep to these rules, and one draw needn't show every extreme that they name: `tile_rows`: local row block of the slot. `tile_cols`: the live slots of one device read exactly one column block from the row blocks of each device; every such device-to-device pair reads at least one. `tile_values`: weights are non-negative; some nodes have no edges.
All inputs are finite; a program needn't handle non-finite values.
Results may differ from a plain program's by a relative error of at most 0.0029.
Values may be sent and summed in bfloat16 or wider, within the bound.
A program may use at most 128 MiB of HBM per device.

v0:
```python
import jax
import jax.numpy as jnp
from jax import lax
from jax.sharding import PartitionSpec as P

DIM = 512
TERMS = 4


epsilon = 1e-12


def local(tile_values, tile_rows, tile_cols, tile_live, degrees, projection, term_weights):
    slot_count = tile_rows.shape[0]
    tile_size = tile_values.shape[1]
    rows_here = degrees.shape[0]
    blocks_dev = rows_here // tile_size
    columns = projection.shape[1]
    living = jnp.arange(slot_count) < tile_live[0]
    owners = ((tile_rows[:, None] == jnp.arange(blocks_dev)[None, :]) & living[:, None]).astype(
        jnp.float32
    )
    row_sums = jnp.sum(tile_values, axis=2, dtype=jnp.float32)
    degree_sum = jnp.einsum("tb,tr->br", owners, row_sums, precision=lax.Precision.HIGHEST)
    inverse = 1.0 / jnp.maximum(degree_sum, 1.0)
    scaling = lax.rsqrt(jnp.maximum(degrees, 1).astype(jnp.float32))
    current = (projection.astype(jnp.float32) * scaling[:, None]).astype(jnp.bfloat16)
    embedding = jnp.zeros((rows_here, columns), jnp.float32)
    for level_index in range(TERMS):
        blocks_local = current.reshape(blocks_dev, tile_size, columns)
        every_block = lax.all_gather(blocks_local, "node", axis=0, tiled=True)
        picked = every_block[tile_cols]
        partial_sum = jnp.einsum(
            "trc,tcd->trd", tile_values, picked, preferred_element_type=jnp.float32
        )
        power_term = jnp.einsum("tb,trd->brd", owners, partial_sum, precision=lax.Precision.HIGHEST)
        power_term = (power_term * inverse[:, :, None]).reshape(rows_here, columns)
        square_local = jnp.sum(power_term * power_term, axis=1)
        square_total = lax.psum(square_local, "col")
        embedding = (
            embedding
            + term_weights[level_index]
            * power_term
            * lax.rsqrt(square_total / DIM + epsilon)[:, None]
        )
        current = power_term.astype(jnp.bfloat16)
    return embedding


def solution(mesh):
    placed = (
        P("node", None, None),
        P("node"),
        P("node"),
        P("node"),
        P("node"),
        P("node", "col"),
        P(),
    )
    return jax.shard_map(
        local, mesh=mesh, in_specs=placed, out_specs=P("node", "col"), check_vma=False
    )
```

profile of v0, /device:TPU:1, one launch (start us, length us, event | category | flops | bytes accessed | tf_op | source)
XLA Modules:
  0.0 486.9 jit_solution(5163505089490957712)
XLA Ops:
  6.5 0.0 all-gather.5.cloned.1.call-start
  6.5 0.7 convert_rsqrt_fusion
  7.2 1.6 copy_bitcast_fusion
  8.8 0.0 all-gather.5.cloned.1.call-update
  8.8 0.0 all-gather.7.cloned.1.call-start
  9.5 0.7 compare_select_fusion
  10.2 1.4 fusion.30
  11.6 0.7 fusion.25
  12.3 7.6 %convert_reduce_fusion = f32[384,128]{1,0:T(8,128)S(1)} fusion(bf16[384,128,128]{2,1,0:T(8,128)(2,1)} %param.7), kind=kLoop, calls=%fused_computation.4 | loop fusion | flops 12533760 | bytes 12779520 | tf_op jit(solution)/shard_map/reduce_sum | solution.py:23
  19.9 0.2 fusion.20
  20.1 67.7 %all-gather.5.cloned.1.call-done = bf16[128,128,64]{1,2,0:T(8,128)(2,1)} async-done(((bf16[4,128,64]{1,2,0:T(8,128)(2,1)}), bf16[128,128,64]{1,2,0:T(8,128)(2,1)}) %all-gather.5.cloned.1.call-update) | async-done | bytes 2097168 | tf_op jit(solution)/shard_map/all_gather | solution.py:31
  87.8 5.6 %gather_fusion = bf16[384,128,64]{1,2,0:T(8,128)(2,1)} fusion(bf16[128,128,64]{1,2,0:T(8,128)(2,1)} %all-gather.5.cloned.1.call-done, s32[1024]{0:T(1024)S(1)} %pad_clamp_fusion), kind=kCustom, calls=%fused_computation | custom fusion | bytes 12584448 | tf_op jit(solution)/shard_map/gather | solution.py:32
  93.4 15.2 %convolution_bitcast_fusion.3 = f32[384,128,64]{1,2,0:T(8,128)} fusion(bf16[384,128,64]{1,2,0:T(8,128)(2,1)} %gather_fusion, bf16[384,128,128]{2,1,0:T(8,128)(2,1)} %param.7), kind=kOutput, calls=%fused_computation.16 | convolution fusion | flops 805306368 | bytes 31457280 | tf_op jit(solution)/shard_map/trc,tcd->trd/dot_general | solution.py:33
  108.6 16.0 %multiply_reduce_fusion.3 = (f32[4,128]{1,0:T(4,128)S(1)}, bf16[4,128,64]{1,0,2:T(4,128)(2,1)S(1)}, f32[4,128,64]{1,0,2:T(4,128)S(1)}) fusion(f32[]{:T(128)} %bitcast, f32[4,128]{1,0:T(4,128)S(1)} %fusion.20, f32[384,128,64]{1,2,0:T(8,128)} %convolution_bitcast_fusion.3, pred[384,4]{0,1:T(4,128)(4,1)S(1)} %fusion.25), kind=kOutput, calls=%fused_computation.33 | convolution fusion | flops 151158272 | bytes 12785156 | tf_op jit(solution)/shard_map/tb,trd->brd/dot_general | solution.py:36
  124.6 0.6 copy.21
  125.2 0.0 all-gather.7.cloned.1.call-update
  125.2 0.5 all-gather.9.cloned.1.call-start
  125.8 74.8 %all-gather.7.cloned.1.call-done = bf16[128,128,64]{1,2,0:T(8,128)(2,1)} async-done(((bf16[4,128,64]{1,2,0:T(8,128)(2,1)}), bf16[128,128,64]{1,2,0:T(8,128)(2,1)}) %all-gather.7.cloned.1.call-update) | async-done | bytes 2097168 | tf_op jit(solution)/shard_map/all_gather | solution.py:31
  200.5 5.6 %gather_fusion.1 = bf16[384,128,64]{1,2,0:T(8,128)(2,1)} fusion(bf16[128,128,64]{1,2,0:T(8,128)(2,1)} %all-gather.7.cloned.1.call-done, s32[1024]{0:T(1024)S(1)} %pad_clamp_fusion), kind=kCustom, calls=%fused_computation.1 | custom fusion | bytes 12584448 | tf_op jit(solution)/shard_map/gather | solution.py:32
  206.1 15.2 %convolution_bitcast_fusion.2 = f32[384,128,64]{1,2,0:T(8,128)} fusion(bf16[384,128,64]{1,2,0:T(8,128)(2,1)} %gather_fusion.1, bf16[384,128,128]{2,1,0:T(8,128)(2,1)} %param.7), kind=kOutput, calls=%fused_computation.15 | convolution fusion | flops 805306368 | bytes 31457280 | tf_op jit(solution)/shard_map/trc,tcd->trd/dot_general | solution.py:33
  221.3 15.9 %multiply_reduce_fusion.2 = (f32[4,128]{1,0:T(4,128)S(1)}, bf16[4,128,64]{1,0,2:T(4,128)(2,1)S(1)}, f32[4,128,64]{1,0,2:T(4,128)S(1)}) fusion(f32[]{:T(128)} %bitcast.5, f32[4,128]{1,0:T(4,128)S(1)} %fusion.20, f32[384,128,64]{1,2,0:T(8,128)} %convolution_bitcast_fusion.2, pred[384,4]{0,1:T(4,128)(4,1)S(1)} %fusion.25), kind=kOutput, calls=%fused_computation.32 | convolution fusion | flops 151158272 | bytes 12785156 | tf_op jit(solution)/shard_map/tb,trd->brd/dot_general | solution.py:36
  237.2 0.6 copy.23
  237.9 0.0 all-gather.9.cloned.1.call-update
  237.9 0.0 all-gather.11.cloned.1.call-start
  238.0 75.2 %all-gather.9.cloned.1.call-done = bf16[128,128,64]{1,2,0:T(8,128)(2,1)} async-done(((bf16[4,128,64]{1,2,0:T(8,128)(2,1)}), bf16[128,128,64]{1,2,0:T(8,128)(2,1)}) %all-gather.9.cloned.1.call-update) | async-done | bytes 2097168 | tf_op jit(solution)/shard_map/all_gather | solution.py:31
  313.2 5.6 %gather_fusion.2 = bf16[384,128,64]{1,2,0:T(8,128)(2,1)} fusion(bf16[128,128,64]{1,2,0:T(8,128)(2,1)} %all-gather.9.cloned.1.call-done, s32[1024]{0:T(1024)S(1)} %pad_clamp_fusion), kind=kCustom, calls=%fused_computation.2 | custom fusion | bytes 12584448 | tf_op jit(solution)/shard_map/gather | solution.py:32
  318.7 15.4 %convolution_bitcast_fusion.1 = f32[384,128,64]{1,2,0:T(8,128)} fusion(bf16[384,128,64]{1,2,0:T(8,128)(2,1)} %gather_fusion.2, bf16[384,128,128]{2,1,0:T(8,128)(2,1)} %param.7), kind=kOutput, calls=%fused_computation.14 | convolution fusion | flops 805306368 | bytes 31457280 | tf_op jit(solution)/shard_map/trc,tcd->trd/dot_general | solution.py:33
  334.1 15.9 %multiply_reduce_fusion.1 = (f32[4,128]{1,0:T(4,128)S(1)}, bf16[4,128,64]{1,0,2:T(4,128)(2,1)S(1)}, f32[4,128,64]{1,0,2:T(4,128)S(1)}) fusion(f32[]{:T(128)} %bitcast.8, f32[4,128]{1,0:T(4,128)S(1)} %fusion.20, f32[384,128,64]{1,2,0:T(8,128)} %convolution_bitcast_fusion.1, pred[384,4]{0,1:T(4,128)(4,1)S(1)} %fusion.25), kind=kOutput, calls=%fused_computation.31 | convolution fusion | flops 151158272 | bytes 12785156 | tf_op jit(solution)/shard_map/tb,trd->brd/dot_general | solution.py:36
  350.0 0.6 copy.25
  350.7 0.0 all-gather.11.cloned.1.call-update
  350.7 75.3 %all-gather.11.cloned.1.call-done = bf16[128,128,64]{1,2,0:T(8,128)(2,1)} async-done(((bf16[4,128,64]{1,2,0:T(8,128)(2,1)}), bf16[128,128,64]{1,2,0:T(8,128)(2,1)}) %all-gather.11.cloned.1.call-update) | async-done | bytes 2097168 | tf_op jit(solution)/shard_map/all_gather | solution.py:31
  426.0 5.6 %gather_fusion.3 = bf16[384,128,64]{1,2,0:T(8,128)(2,1)} fusion(bf16[128,128,64]{1,2,0:T(8,128)(2,1)} %all-gather.11.cloned.1.call-done, s32[1024]{0:T(1024)S(1)} %pad_clamp_fusion), kind=kCustom, calls=%fused_computation.3 | custom fusion | bytes 12584448 | tf_op jit(solution)/shard_map/gather | solution.py:32
  431.6 15.2 %convolution_bitcast_fusion = f32[384,128,64]{1,2,0:T(8,128)} fusion(bf16[384,128,64]{1,2,0:T(8,128)(2,1)} %gather_fusion.3, bf16[384,128,128]{2,1,0:T(8,128)(2,1)} %param.7), kind=kOutput, calls=%fused_computation.13 | convolution fusion | flops 805306368 | bytes 31457280 | tf_op jit(solution)/shard_map/trc,tcd->trd/dot_general | solution.py:33
  446.8 16.1 %multiply_reduce_fusion = (f32[4,128]{1,0:T(4,128)S(1)}, f32[4,128,64]{1,0,2:T(4,128)S(1)}) fusion(f32[]{:T(128)} %bitcast.11, f32[4,128]{1,0:T(4,128)S(1)} %fusion.20, f32[384,128,64]{1,2,0:T(8,128)} %convolution_bitcast_fusion, pred[384,4]{0,1:T(4,128)(4,1)S(1)} %fusion.25), kind=kOutput, calls=%fused_computation.30 | convolution fusion | flops 151125504 | bytes 12719620 | tf_op jit(solution)/shard_map/tb,trd->brd/dot_general | solution.py:36
  462.9 16.5 %all-reduce = (f32[512]{0:T(512)S(1)}, f32[512]{0:T(512)S(1)}, f32[512]{0:T(512)S(1)}, f32[512]{0:T(512)S(1)}) all-reduce(f32[512]{0:T(512)S(1)} %bitcast.89, f32[512]{0:T(512)S(1)} %bitcast.88, f32[512]{0:T(512)S(1)} %bitcast.87, f32[512]{0:T(512)S(1)} %bitcast.86), channel_id=1, replica_groups=mesh['node'=32,'col'=8] {'col'}, use_global_device_ids=true, to_apply=%region_8.0 | all-reduce | flops 2048 | bytes 16384 | tf_op jit(solution)/shard_map/psum | solution.py:39
  479.4 0.7 fusion.21
  (4 shorter events, 0.0 us)
Async XLA Ops:
  6.5 81.3 %all-gather.5.cloned.1.call-start = ((), (), s32[]{:S(2)}) async-start(), calls=%async_computation | async-start | bytes 2162688 | tf_op jit(solution)/shard_map/all_gather | solution.py:31
  8.8 191.7 %all-gather.7.cloned.1.call-start = ((), (), s32[]{:S(2)}) async-start(), calls=%async_computation.1 | async-start | bytes 2162688 | tf_op jit(solution)/shard_map/all_gather | solution.py:31
  125.2 188.0 %all-gather.9.cloned.1.call-start = ((), (), s32[]{:S(2)}) async-start(), calls=%async_computation.2 | async-start | bytes 2162688 | tf_op jit(solution)/shard_map/all_gather | solution.py:31
  237.9 188.1 %all-gather.11.cloned.1.call-start = ((), (), s32[]{:S(2)}) async-start(), calls=%async_computation.3 | async-start | bytes 2162688 | tf_op jit(solution)/shard_map/all_gather | solution.py:31
Sparse Core Ops, SparseCore 0:
  9.9 77.8 all-gather.4
  125.4 75.1 all-gather.6
  238.0 75.1 all-gather.8
  350.8 75.1 all-gather.10
where the time goes:
time: 495 us; the launch traced here: 487 us
  waiting for transfers between devices  293 us (59%)
  matrix products  125 us (25%)
  local copies, waits for them, and re-layouts  25.5 us (5%)
  blocking collectives  16.5 us (3%)
  between operations  14.1 us (3%)
  other arithmetic  11.9 us (2%)
    all_gather x4, waiting for transfers between devices, local(): every_block = lax.all_gather(blocks_local, 'node', axis=0, tiled=True)  293 us
    dot_general x4, matrix products, local(): jnp.einsum('tb,trd->brd', owners, partial_sum, precision=lax.Precision.HI...  63.9 us
    dot_general x4, matrix products, local(): jnp.einsum('trc,tcd->trd', tile_values, picked, preferred_element_type=jn...  61.1 us
    gather x4, local copies, waits for them, and re-layouts, local(): picked = every_block[tile_cols]  22.2 us
    psum x1, blocking collectives, local(): square_total = lax.psum(square_local, 'col')  16.5 us
  transfers between devices with their start and end apart: 4, of which 4 were waited for; matrix products, arithmetic and copies ran while one was open for 2% of the time, Pallas kernels for 0%

commit v1 on v0

v1 whole, which is shorter than its diff:
```python
import functools

import jax
import jax.numpy as jnp
from jax import lax
from jax.experimental import pallas as pl
from jax.experimental.pallas import tpu as pltpu
from jax.sharding import PartitionSpec as P

MESH = pl.DeviceIdType.MESH
DIM = 512
TERMS = 4
TILE = 128
BLOCKS = 4
SLOTS = 384
NY, NZ = 4, 8
NODES = NY * NZ
COLS = 8
HALVES = 2
WIDTH = DIM // COLS // HALVES
ROWS = BLOCKS * TILE
EPSILON = 1e-12
CHUNKS = 4

PLACE = (0, 1, 3, 5, 7, 6, 4, 2)
GROUPS = ((0, 12), (12, 8), (20, 8), (28, 4))


def slot_of(dy, dz):
    return PLACE[dz % NZ] * NY + dy % NY


OFFSETS = [
    (dy, dz) for dz in (4, 3, 5, 2, 6, 1, 7, 0) for dy in (2, 1, 3, 0) if (dy, dz) != (0, 0)
]


def group_of(slot):
    return [g for g, (first, count) in enumerate(GROUPS) if first <= slot < first + count][0]


def column(row):
    return jnp.transpose(jnp.broadcast_to(row, (TILE, TILE)))


def kernel(
    rows_ref, cols_ref, live_ref, degrees_ref, weights_ref, projection_hbm, values_hbm,
    out_ref,
    tiles, sums, matrix, gathered, staged, current, powers, squares, projected,
    meta_vmem, meta, wanted_vmem, wanted,
    tile_sem, local_sem, need_send, need_recv, send_sem, recv_sem, square_send, square_recv,
):
    node = lax.axis_index("node")
    col = lax.axis_index("col")
    y = node // NZ
    z = node - y * NZ

    def peer(dy, dz):
        return {"node": lax.rem(y + dy, NY) * NZ + lax.rem(z + dz, NZ), "col": col}

    def col_peer(d):
        return {"node": node, "col": lax.rem(col + d, COLS)}

    per = SLOTS // CHUNKS

    def load_tiles(i):
        part = pl.ds(i * per, per)
        return pltpu.make_async_copy(values_hbm.at[part], tiles.at[part], tile_sem.at[i])

    load_projection = pltpu.make_async_copy(projection_hbm, projected, local_sem.at[0])
    load_projection.start()
    for i in range(CHUNKS):
        load_tiles(i).start()

    barrier = pltpu.get_barrier_semaphore()
    for dy, dz in OFFSETS:
        pl.semaphore_signal(barrier, inc=1, device_id=peer(dy, dz), device_id_type=MESH)
    for d in range(1, COLS):
        pl.semaphore_signal(barrier, inc=1, device_id=col_peer(d), device_id_type=MESH)

    cols = cols_ref[...]
    token = lax.broadcasted_iota(jnp.int32, (3, TILE), 0) * TILE + lax.broadcasted_iota(
        jnp.int32, (3, TILE), 1
    )
    dy = ((cols >> 5) - y) & (NY - 1)
    dz = (((cols >> 2) & (NZ - 1)) - z) & (NZ - 1)
    place = jnp.where(dz <= NZ // 2, jnp.maximum(2 * dz - 1, 0), 2 * (NZ - dz))
    key = ((rows_ref[...] * NODES + place * NY + dy) * BLOCKS + (cols & (BLOCKS - 1))) * 512
    key = jnp.where(token < live_ref[0], key, TILE * BLOCKS * 512) + token
    lane = lax.broadcasted_iota(jnp.int32, (1, TILE), 1)
    tall = lax.broadcasted_iota(jnp.int32, (TILE, 1), 0)
    key_col = [column(key[c : c + 1]) for c in range(3)]
    rank = [
        sum(
            jnp.sum((key_col[b] < key[c : c + 1]).astype(jnp.int32), axis=0, keepdims=True)
            for b in range(3)
        )
        for c in range(3)
    ]
    rank_col = [column(rank[c]) for c in range(3)]
    pair_col = [k >> 11 for k in key_col]

    def pick(position, what):
        return sum(
            jnp.sum(jnp.where(rank_col[b] == position, what[b], 0), axis=0, keepdims=True)
            for b in range(3)
        )

    token_col = [jnp.broadcast_to(tall + b * TILE, (TILE, TILE)) for b in range(3)]
    for c in range(3):
        position = lane + c * TILE
        meta_vmem[c : c + 1] = pick(position, token_col)
        same = pick(position, pair_col) == pick(position - 1, pair_col)
        meta_vmem[3 + c : 4 + c] = (same & (position > 0)).astype(jnp.int32)
    upto = sum(jnp.sum((k <= lane).astype(jnp.int32), axis=0, keepdims=True) for k in pair_col)
    below = sum(jnp.sum((k < lane).astype(jnp.int32), axis=0, keepdims=True) for k in pair_col)
    meta_vmem[6:7] = jnp.maximum(upto - 1, 0)
    meta_vmem[7:8] = (upto > below).astype(jnp.int32)
    wanted_block = [
        jnp.where(
            (k < TILE * BLOCKS * 512) & (((k >> 11) & (NODES - 1)) == lane),
            (k >> 9) & (BLOCKS - 1),
            0,
        )
        for k in key_col
    ]
    need = functools.reduce(
        jnp.maximum, [jnp.max(w, axis=0, keepdims=True) for w in wanted_block]
    )
    wanted_vmem[0] = need
    load_meta = pltpu.make_async_copy(meta_vmem, meta, local_sem.at[1])
    load_meta.start()

    load_projection.wait()
    scaling = lax.rsqrt(jnp.maximum(degrees_ref[...], 1).astype(jnp.float32))
    for b in range(BLOCKS):
        block = projected[b * TILE : (b + 1) * TILE, :].astype(jnp.float32)
        block = jnp.transpose(block) * scaling[b : b + 1]
        for h in range(HALVES):
            current[h, b] = block[h * WIDTH : (h + 1) * WIDTH].astype(jnp.bfloat16)

    pl.semaphore_wait(barrier, len(OFFSETS) + COLS - 1)

    for dy, dz in OFFSETS:
        pltpu.make_async_remote_copy(
            src_ref=wanted_vmem.at[0],
            dst_ref=wanted_vmem.at[slot_of(-dy, -dz)],
            send_sem=need_send,
            recv_sem=need_recv,
            device_id=peer(dy, dz),
            device_id_type=MESH,
        ).start()

    for i in range(CHUNKS):
        load_tiles(i).wait()
    load_meta.wait()

    def add_tiles(c, acc):
        def add(i, acc):
            keep = meta[3 + c, i].astype(jnp.float32)
            acc = acc * keep + tiles[meta[c, i]].astype(jnp.float32)
            sums[c * TILE + i] = acc.astype(jnp.bfloat16)
            return acc

        return lax.fori_loop(0, TILE, add, acc, unroll=2)

    def need_copies():
        others = wanted_vmem.at[pl.ds(1, NODES - 1)]
        return pltpu.make_async_remote_copy(
            src_ref=others, dst_ref=others, send_sem=need_send, recv_sem=need_recv,
            device_id=peer(0, 1), device_id_type=MESH,
        )

    def send(k, h):
        for dy, dz in OFFSETS:
            to, at = slot_of(dy, dz), slot_of(-dy, -dz)
            staged[k, h, to] = current[h, wanted[to, 0, at]]
            pltpu.make_async_remote_copy(
                src_ref=staged.at[k, h, to],
                dst_ref=gathered.at[k, h, at],
                send_sem=send_sem.at[k, h],
                recv_sem=recv_sem.at[k, h, group_of(at)],
                device_id=peer(dy, dz),
                device_id_type=MESH,
            ).start()
        gathered[k, h, 0] = current[h, wanted[0, 0, 0]]

    def group_copies(k, h, first, count, g):
        part = gathered.at[k, h, pl.ds(first, count)]
        return pltpu.make_async_remote_copy(
            src_ref=part, dst_ref=part, send_sem=send_sem.at[k, h], recv_sem=recv_sem.at[k, h, g],
            device_id=peer(0, 1), device_id_type=MESH,
        )

    acc = add_tiles(0, jnp.zeros((TILE, TILE), jnp.float32))
    need_copies().wait_recv()
    load_wanted = pltpu.make_async_copy(wanted_vmem, wanted, local_sem.at[2])
    load_wanted.start()
    load_wanted.wait()
    for h in range(HALVES):
        send(0, h)
    acc = add_tiles(1, acc)
    acc = add_tiles(2, acc)

    def place_block(s, _):
        for r in range(BLOCKS):
            pair = r * NODES + s
            block = sums[meta[6, pair]] * meta[7, pair].astype(jnp.bfloat16)
            matrix[r * TILE : (r + 1) * TILE, pl.ds(pl.multiple_of(s * TILE, TILE), TILE)] = block
        return 0

    lax.fori_loop(0, NODES, place_block, 0)

    def times(x, first, count):
        part = matrix[:, first * TILE : (first + count) * TILE]
        return lax.dot_general(
            x, part, (((1,), (1,)), ((), ())), preferred_element_type=jnp.float32
        )

    ones = jnp.ones((16, TILE * 8), jnp.bfloat16)
    row_sum = sum(times(ones, first, 8) for first in range(0, NODES, 8))[0:1]
    inverse = 1.0 / jnp.maximum(row_sum, 1.0)

    def square_copies(k):
        others = squares.at[k, pl.ds(1, COLS - 1)]
        return pltpu.make_async_remote_copy(
            src_ref=others, dst_ref=others, send_sem=square_send.at[k],
            recv_sem=square_recv.at[k], device_id=col_peer(1), device_id_type=MESH,
        )

    for k in range(TERMS):
        square = jnp.zeros((1, ROWS), jnp.float32)
        for h in range(HALVES):
            power = jnp.zeros((WIDTH, ROWS), jnp.float32)
            for g, (first, count) in enumerate(GROUPS):
                skip = 1 if first == 0 else 0
                group_copies(k, h, first + skip, count - skip, g).wait_recv()
                x = jnp.concatenate([gathered[k, h, first + i] for i in range(count)], axis=1)
                power = power + times(x, first, count)
            power = power * inverse
            if k < TERMS - 1:
                for b in range(BLOCKS):
                    current[h, b] = power[:, b * TILE : (b + 1) * TILE].astype(jnp.bfloat16)
                send(k + 1, h)
            powers[k, h * WIDTH : (h + 1) * WIDTH] = power
            square = square + jnp.sum(power * power, axis=0, keepdims=True)
        squares[k, 0] = square
        for d in range(1, COLS):
            pltpu.make_async_remote_copy(
                src_ref=squares.at[k, 0],
                dst_ref=squares.at[k, COLS - d],
                send_sem=square_send.at[k],
                recv_sem=square_recv.at[k],
                device_id=col_peer(d),
                device_id_type=MESH,
            ).start()

    embedding = jnp.zeros((HALVES * WIDTH, ROWS), jnp.float32)
    for k in range(TERMS):
        square_copies(k).wait_recv()
        square = functools.reduce(jnp.add, [squares[k, d] for d in range(COLS)])
        factor = weights_ref[k] * lax.rsqrt(square * (1.0 / DIM) + EPSILON)
        embedding = embedding + powers[k] * factor
    out_ref[...] = embedding

    need_copies().wait_send()
    for k in range(TERMS):
        square_copies(k).wait_send()
        for h in range(HALVES):
            group_copies(k, h, 1, NODES - 1, 0).wait_send()


def local(tile_values, tile_rows, tile_cols, tile_live, degrees, projection, term_weights):
    vmem = pl.BlockSpec(memory_space=pltpu.VMEM)
    smem = pl.BlockSpec(memory_space=pltpu.SMEM)
    anywhere = pl.BlockSpec(memory_space=pl.ANY)
    width = HALVES * WIDTH
    bf16, f32, i32 = jnp.bfloat16, jnp.float32, jnp.int32
    out = pl.pallas_call(
        kernel,
        out_shape=jax.ShapeDtypeStruct((width, ROWS), f32),
        in_specs=[vmem, vmem, smem, vmem, smem, anywhere, anywhere],
        out_specs=vmem,
        scratch_shapes=[
            pltpu.VMEM((SLOTS, TILE, TILE), bf16),
            pltpu.VMEM((SLOTS, TILE, TILE), bf16),
            pltpu.VMEM((ROWS, NODES * TILE), bf16),
            pltpu.VMEM((TERMS, HALVES, NODES, WIDTH, TILE), bf16),
            pltpu.VMEM((TERMS, HALVES, NODES, WIDTH, TILE), bf16),
            pltpu.VMEM((HALVES, BLOCKS, WIDTH, TILE), bf16),
            pltpu.VMEM((TERMS, width, ROWS), f32),
            pltpu.VMEM((TERMS, COLS, 1, ROWS), f32),
            pltpu.VMEM((ROWS, width), i32),
            pltpu.VMEM((8, TILE), i32),
            pltpu.SMEM((8, TILE), i32),
            pltpu.VMEM((NODES, 1, TILE), i32),
            pltpu.SMEM((NODES, 1, TILE), i32),
            pltpu.SemaphoreType.DMA((CHUNKS,)),
            pltpu.SemaphoreType.DMA((3,)),
            pltpu.SemaphoreType.DMA,
            pltpu.SemaphoreType.DMA,
            pltpu.SemaphoreType.DMA((TERMS, HALVES)),
            pltpu.SemaphoreType.DMA((TERMS, HALVES, len(GROUPS))),
            pltpu.SemaphoreType.DMA((TERMS,)),
            pltpu.SemaphoreType.DMA((TERMS,)),
        ],
        compiler_params=pltpu.CompilerParams(
            collective_id=0, has_side_effects=True, vmem_limit_bytes=52 << 20
        ),
        cost_estimate=pl.CostEstimate(
            flops=2 * TERMS * width * ROWS * NODES * TILE,
            bytes_accessed=SLOTS * TILE * TILE * 2,
            transcendentals=0,
        ),
        name="embed",
    )(
        tile_rows.reshape(3, TILE),
        tile_cols.reshape(3, TILE),
        tile_live,
        degrees.reshape(BLOCKS, TILE),
        term_weights,
        projection,
        tile_values,
    )
    return out.T


def solution(mesh):
    placed = (
        P("node", None, None),
        P("node"),
        P("node"),
        P("node"),
        P("node"),
        P("node", "col"),
        P(),
    )
    return jax.shard_map(
        local, mesh=mesh, in_specs=placed, out_specs=P("node", "col"), check_vma=False
    )
```

time: 495 us -> 77 us (0.16); the launches traced: 487 us -> 76.8 us
  waiting for transfers between devices: 293 us -> 0 us
  matrix products: 125 us -> 0 us
  Pallas kernels: 0 us -> 71.7 us
  local copies, waits for them, and re-layouts: 25.5 us -> 4.38 us
  blocking collectives: 16.5 us -> 0 us
  between operations: 14.1 us -> 0.68 us
  other arithmetic: 11.9 us -> 0 us
    all_gather x4 -> x0, waiting for transfers between devices: 293 us -> none  [local(): every_block = lax.all_gather(blocks_local, 'node', axis=0, tiled=True)]
    dot_general x9 -> x0, matrix products: 125 us -> none  [the longest x4 63.9 us: local(): jnp.einsum('tb,trd->brd', owners, partial_sum, precision=lax.Precision.HI...]
    pallas_call x0 -> x1, Pallas kernels: none -> 71.7 us  [local(): pl.pallas_call(kernel, out_shape=jax.ShapeDtypeStruct((width, ROWS), f32)...]
    gather x4 -> x0, local copies, waits for them, and re-layouts: 22.2 us -> none  [local(): picked = every_block[tile_cols]]
    psum x1 -> x0, blocking collectives: 16.5 us -> none  [local(): square_total = lax.psum(square_local, 'col')]
    reduce_sum x1 -> x0, other arithmetic: 7.6 us -> none  [local(): row_sums = jnp.sum(tile_values, axis=2, dtype=jnp.float32)]
  transfers between devices with their start and end apart: 4 -> 0, of which waited for: 4 -> 0; matrix products, arithmetic and copies ran while one was open for 2% -> 0% of each run, Pallas kernels for 0% -> 0%
where the time goes in v1:
time: 77 us; the launch traced here: 76.8 us
  Pallas kernels  71.7 us (93%)
  local copies, waits for them, and re-layouts  4.38 us (6%)
    pallas_call x1, Pallas kernels, local(): pl.pallas_call(kernel, out_shape=jax.ShapeDtypeStruct((width, ROWS), f32)...  71.7 us
    unnamed x10, local copies, waits for them, and re-layouts  4.38 us

profile of v1, /device:TPU:1, one launch (start us, length us, event | category | flops | bytes accessed | tf_op | source)
XLA Modules:
  0.0 76.8 jit_solution(1453034835639434604)
XLA Ops:
  0.7 1.0 %copy.8.projection_hbm = s32[512,64]{1,0:T(8,128)S(1)} copy(s32[512,64]{0,1:T(8,128)} %param.12) | data formatting | bytes 262144 | tf_op args[5]
  1.7 0.0 copy-start
  1.7 0.7 copy-done
  2.4 0.0 copy-start.1
  2.4 0.7 copy-done.1
  3.1 0.0 copy-start.2
  3.1 0.7 copy-done.2
  3.7 0.0 copy-start.3
  3.7 0.7 copy-done.3
  4.4 71.7 %embed.1 = f32[64,512]{1,0:T(8,128)S(1)} custom-call(s32[3,128]{1,0:T(4,128)S(1)} %bitcast.5, s32[3,128]{1,0:T(4,128)S(1)} %bitcast.6, s32[1]{0:T(128)S(6)} %copy.10.live_ref, s32[4,128]{1,0:T(4,128)S(1)} %bitcast.7, f32[4]{0:T(128)S(1)} %copy-done.3, s32[512,64]{1,0:T(8,128)S(1)} %copy.8.projection_hbm, bf16[384,128,128]{2,1,0:T(8,128)(2,1)} %values_hbm.1), custom_call_target="tpu_custom_call" | custom-call | flops 1073741824 | bytes 12582912 | tf_op jit(solution)/shard_map/embed/pallas_call | solution.py:279
  76.1 0.7 copy.11
Async XLA Ops:
  1.7 0.7 copy-start
  2.4 0.7 copy-start.1
  3.1 0.7 copy-start.2
  3.7 0.7 copy-start.3

commit v2 on v1

v2 whole, which is shorter than its diff:
```python
import functools

import jax
import jax.numpy as jnp
from jax import lax
from jax.experimental import pallas as pl
from jax.experimental.pallas import tpu as pltpu
from jax.sharding import PartitionSpec as P

MESH = pl.DeviceIdType.MESH
DIM = 512
TERMS = 4
TILE = 128
BLOCKS = 4
SLOTS = 384
NY, NZ = 4, 8
NODES = NY * NZ
COLS = 8
HALVES = 2
WIDTH = DIM // COLS // HALVES
ROWS = BLOCKS * TILE
EPSILON = 1e-12
CHUNKS = 4

PLACE = (0, 1, 3, 5, 7, 6, 4, 2)
GROUPS = ((0, 12), (12, 8), (20, 8), (28, 4))


def slot_of(dy, dz):
    return PLACE[dz % NZ] * NY + dy % NY


def turned(offset):
    return -offset[0], -offset[1]


DIRECT = [(dy, dz) for dz in (0, 1, -1) for dy in (2, 1, 3, 0) if (dy, dz) != (0, 0)]
HUBS = (2, -2)
READERS = {
    2: [(0, 2), (1, 2)] + [(dy, 1) for dy in (2, 1, 3, 0)] + [(2, 0), (1, 0), (3, 0)],
    -2: [(2, -2), (3, -2)] + [(dy, -1) for dy in (2, 1, 3, 0)] + [(2, 0), (1, 0), (3, 0)],
}
NEAR = [(dy, dz) for dz in (2, -2, 1, -1, 0) for dy in (2, 1, 3, 0) if (dy, dz) != (0, 0)]
KNOWN = len(NEAR) + 1
MESSAGES = len(DIRECT) + 2 * len(READERS[2])
ARRIVING = (11, 6, 8, 4)


def group_of(slot):
    return [g for g, (first, count) in enumerate(GROUPS) if first <= slot < first + count][0]


def column(row):
    return jnp.transpose(jnp.broadcast_to(row, (TILE, TILE)))


def kernel(
    rows_hbm, cols_hbm, live_ref, degrees_hbm, weights_ref, projection_hbm, values_hbm,
    out_ref,
    rows_ref, cols_ref, degrees_ref,
    tiles, sums, matrix, hub, held, relayed, gathered, staged, current, powers, squares, projected,
    meta_vmem, meta, wanted_vmem, wanted,
    tile_sem, local_sem, need_send, need_recv, hub_send, hub_recv, send_sem, recv_sem,
    square_send, square_recv,
):
    node = lax.axis_index("node")
    col = lax.axis_index("col")
    y = node // NZ
    z = node - y * NZ

    def peer(offset):
        dy, dz = offset
        return {"node": lax.rem(y + dy, NY) * NZ + lax.rem(z + dz + NZ, NZ), "col": col}

    def col_peer(d):
        return {"node": node, "col": lax.rem(col + d, COLS)}

    per = SLOTS // CHUNKS

    def load_tiles(i):
        part = pl.ds(i * per, per)
        return pltpu.make_async_copy(values_hbm.at[part], tiles.at[part], tile_sem.at[i])

    loads = [
        pltpu.make_async_copy(src, dst, local_sem.at[i])
        for i, (src, dst) in enumerate(
            [
                (cols_hbm, cols_ref),
                (rows_hbm, rows_ref),
                (degrees_hbm, degrees_ref),
                (projection_hbm, projected),
            ]
        )
    ]
    for load in loads:
        load.start()
    barrier = pltpu.get_barrier_semaphore()
    for offset in NEAR:
        pl.semaphore_signal(barrier, inc=1, device_id=peer(offset), device_id_type=MESH)
    for d in range(1, COLS):
        pl.semaphore_signal(barrier, inc=1, device_id=col_peer(d), device_id_type=MESH)
    for i in range(CHUNKS):
        load_tiles(i).start()
    for load in loads:
        load.wait()

    scaling = lax.rsqrt(jnp.maximum(degrees_ref[...], 1).astype(jnp.float32))
    for b in range(BLOCKS):
        block = projected[:, b * TILE : (b + 1) * TILE].astype(jnp.float32)
        block = block * scaling[b : b + 1]
        for h in range(HALVES):
            current[0, h, b] = block[h * WIDTH : (h + 1) * WIDTH].astype(jnp.bfloat16)

    cols = cols_ref[...]
    token = lax.broadcasted_iota(jnp.int32, (3, TILE), 0) * TILE + lax.broadcasted_iota(
        jnp.int32, (3, TILE), 1
    )
    dy = ((cols >> 5) - y) & (NY - 1)
    dz = (((cols >> 2) & (NZ - 1)) - z) & (NZ - 1)
    place = jnp.where(dz <= NZ // 2, jnp.maximum(2 * dz - 1, 0), 2 * (NZ - dz))
    key = ((rows_ref[...] * NODES + place * NY + dy) * BLOCKS + (cols & (BLOCKS - 1))) * 512
    key = jnp.where(token < live_ref[0], key, TILE * BLOCKS * 512) + token
    lane = lax.broadcasted_iota(jnp.int32, (1, TILE), 1)
    tall = lax.broadcasted_iota(jnp.int32, (TILE, 1), 0)
    key_col = [column(key[c : c + 1]) for c in range(3)]
    wanted_block = [
        jnp.where(
            (k < TILE * BLOCKS * 512) & (((k >> 11) & (NODES - 1)) == lane),
            (k >> 9) & (BLOCKS - 1),
            0,
        )
        for k in key_col
    ]
    wanted_vmem[0] = functools.reduce(
        jnp.maximum, [jnp.max(w, axis=0, keepdims=True) for w in wanted_block]
    )

    def need_copy(offset):
        return pltpu.make_async_remote_copy(
            src_ref=wanted_vmem.at[0],
            dst_ref=wanted_vmem.at[slot_of(*turned(offset))],
            send_sem=need_send,
            recv_sem=need_recv,
            device_id=peer(offset),
            device_id_type=MESH,
        )

    def need_copies():
        others = wanted_vmem.at[pl.ds(1, KNOWN - 1)]
        return pltpu.make_async_remote_copy(
            src_ref=others, dst_ref=others, send_sem=need_send, recv_sem=need_recv,
            device_id=peer((0, 1)), device_id_type=MESH,
        )

    def hub_copy(k, h, i):
        return pltpu.make_async_remote_copy(
            src_ref=current.at[k, h],
            dst_ref=hub.at[k, h, i],
            send_sem=hub_send.at[k, h, i],
            recv_sem=hub_recv.at[k, h, i],
            device_id=peer((0, HUBS[i])),
            device_id_type=MESH,
        )

    def send_hubs(k, h):
        for i in range(2):
            hub_copy(k, h, i).start()

    pl.semaphore_wait(barrier, len(NEAR) + COLS - 1)
    for h in range(HALVES):
        send_hubs(0, h)
    for offset in NEAR:
        need_copy(offset).start()

    rank = [
        sum(
            jnp.sum((key_col[b] < key[c : c + 1]).astype(jnp.int32), axis=0, keepdims=True)
            for b in range(3)
        )
        for c in range(3)
    ]
    rank_col = [column(rank[c]) for c in range(3)]
    pair_col = [k >> 11 for k in key_col]

    def pick(position, what):
        return sum(
            jnp.sum(jnp.where(rank_col[b] == position, what[b], 0), axis=0, keepdims=True)
            for b in range(3)
        )

    token_col = [jnp.broadcast_to(tall + b * TILE, (TILE, TILE)) for b in range(3)]
    for c in range(3):
        position = lane + c * TILE
        meta_vmem[c : c + 1] = pick(position, token_col)
        same = pick(position, pair_col) == pick(position - 1, pair_col)
        meta_vmem[3 + c : 4 + c] = (same & (position > 0)).astype(jnp.int32)
    upto = sum(jnp.sum((k <= lane).astype(jnp.int32), axis=0, keepdims=True) for k in pair_col)
    below = sum(jnp.sum((k < lane).astype(jnp.int32), axis=0, keepdims=True) for k in pair_col)
    meta_vmem[6:7] = jnp.maximum(upto - 1, 0)
    meta_vmem[7:8] = (upto > below).astype(jnp.int32)
    load_meta = pltpu.make_async_copy(meta_vmem, meta, local_sem.at[6])
    load_meta.start()
    for i in range(CHUNKS):
        load_tiles(i).wait()
    load_meta.wait()

    def add_tiles(c, acc):
        def add(i, acc):
            keep = meta[3 + c, i].astype(jnp.float32)
            acc = acc * keep + tiles[meta[c, i]].astype(jnp.float32)
            sums[c * TILE + i] = acc.astype(jnp.bfloat16)
            return acc

        return lax.fori_loop(0, TILE, add, acc, unroll=4)

    def send(k, h):
        for offset in DIRECT:
            to, at = slot_of(*offset), slot_of(*turned(offset))
            staged[k, h, to] = current[k, h, wanted[to, 0, at]]
        gathered[k, h, 0] = current[k, h, wanted[0, 0, 0]]
        for offset in DIRECT:
            to, at = slot_of(*offset), slot_of(*turned(offset))
            pltpu.make_async_remote_copy(
                src_ref=staged.at[k, h, to],
                dst_ref=gathered.at[k, h, at],
                send_sem=send_sem.at[k, h],
                recv_sem=recv_sem.at[k, h, group_of(at)],
                device_id=peer(offset),
                device_id_type=MESH,
            ).start()

    def relay(k, h):
        for i, d in enumerate(HUBS):
            hub_copy(k, h, i).wait_recv()
            held[i] = hub[k, h, i]
            places = [slot_of(-dy, -d - dz) for dy, dz in READERS[d]]
            for j, offset in enumerate(READERS[d]):
                relayed[k, h, i, j] = held[i, wanted[slot_of(*offset), 0, places[j]]]
            own = slot_of(0, -d)
            gathered[k, h, own] = held[i, wanted[0, 0, own]]
            for j, offset in enumerate(READERS[d]):
                pltpu.make_async_remote_copy(
                    src_ref=relayed.at[k, h, i, j],
                    dst_ref=gathered.at[k, h, places[j]],
                    send_sem=send_sem.at[k, h],
                    recv_sem=recv_sem.at[k, h, group_of(places[j])],
                    device_id=peer(offset),
                    device_id_type=MESH,
                ).start()

    def group_copies(k, h, count, g):
        part = gathered.at[k, h, pl.ds(0, count)]
        return pltpu.make_async_remote_copy(
            src_ref=part, dst_ref=part, send_sem=send_sem.at[k, h], recv_sem=recv_sem.at[k, h, g],
            device_id=peer((0, 1)), device_id_type=MESH,
        )

    acc = add_tiles(0, jnp.zeros((TILE, TILE), jnp.float32))
    need_copies().wait_recv()
    load_wanted = pltpu.make_async_copy(wanted_vmem, wanted, local_sem.at[7])
    load_wanted.start()
    load_wanted.wait()
    for h in range(HALVES):
        send(0, h)
    for h in range(HALVES):
        relay(0, h)
    acc = add_tiles(1, acc)
    acc = add_tiles(2, acc)

    def place_block(s, _):
        for r in range(BLOCKS):
            pair = r * NODES + s
            block = sums[meta[6, pair]] * meta[7, pair].astype(jnp.bfloat16)
            matrix[r * TILE : (r + 1) * TILE, pl.ds(pl.multiple_of(s * TILE, TILE), TILE)] = block
        return 0

    lax.fori_loop(0, NODES, place_block, 0)

    def times(x, first, count):
        part = matrix[:, first * TILE : (first + count) * TILE]
        return lax.dot_general(
            x, part, (((1,), (1,)), ((), ())), preferred_element_type=jnp.float32
        )

    def square_copies(k):
        others = squares.at[k, pl.ds(1, COLS - 1)]
        return pltpu.make_async_remote_copy(
            src_ref=others, dst_ref=others, send_sem=square_send.at[k],
            recv_sem=square_recv.at[k], device_id=col_peer(1), device_id_type=MESH,
        )

    def product(k, h):
        power = jnp.zeros((WIDTH + 16, ROWS), jnp.float32)
        for g, (first, count) in enumerate(GROUPS):
            group_copies(k, h, ARRIVING[g], g).wait_recv()
            x = jnp.concatenate([gathered[k, h, first + i] for i in range(count)], axis=1)
            x = jnp.concatenate([x, jnp.ones((16, count * TILE), jnp.bfloat16)], axis=0)
            power = power + times(x, first, count)
        power = power[:WIDTH] * (1.0 / jnp.maximum(power[WIDTH : WIDTH + 1], 1.0))
        powers[k, h * WIDTH : (h + 1) * WIDTH] = power
        return power

    def send_squares(k, parts):
        squares[k, 0] = sum(jnp.sum(p * p, axis=0, keepdims=True) for p in parts)
        for d in range(1, COLS):
            pltpu.make_async_remote_copy(
                src_ref=squares.at[k, 0],
                dst_ref=squares.at[k, COLS - d],
                send_sem=square_send.at[k],
                recv_sem=square_recv.at[k],
                device_id=col_peer(d),
                device_id_type=MESH,
            ).start()

    for k in range(TERMS):
        parts = []
        for h in range(HALVES):
            power = product(k, h)
            parts.append(power)
            if k < TERMS - 1:
                for b in range(BLOCKS):
                    part = power[:, b * TILE : (b + 1) * TILE]
                    current[k + 1, h, b] = part.astype(jnp.bfloat16)
                send_hubs(k + 1, h)
                send(k + 1, h)
        if k < TERMS - 1:
            for h in range(HALVES):
                relay(k + 1, h)
        send_squares(k, parts)

    embedding = jnp.zeros((HALVES * WIDTH, ROWS), jnp.float32)
    for k in range(TERMS):
        square_copies(k).wait_recv()
        square = functools.reduce(jnp.add, [squares[k, d] for d in range(COLS)])
        factor = weights_ref[k] * lax.rsqrt(square * (1.0 / DIM) + EPSILON)
        embedding = embedding + powers[k] * factor
    out_ref[...] = embedding

    need_copies().wait_send()
    for k in range(TERMS):
        square_copies(k).wait_send()
        for h in range(HALVES):
            group_copies(k, h, MESSAGES, 0).wait_send()
            for i in range(2):
                hub_copy(k, h, i).wait_send()


def local(tile_values, tile_rows, tile_cols, tile_live, degrees, projection, term_weights):
    vmem = pl.BlockSpec(memory_space=pltpu.VMEM)
    smem = pl.BlockSpec(memory_space=pltpu.SMEM)
    anywhere = pl.BlockSpec(memory_space=pl.ANY)
    width = HALVES * WIDTH
    bf16, f32, i32 = jnp.bfloat16, jnp.float32, jnp.int32
    out = pl.pallas_call(
        kernel,
        out_shape=jax.ShapeDtypeStruct((width, ROWS), f32),
        in_specs=[anywhere, anywhere, smem, anywhere, smem, anywhere, anywhere],
        out_specs=vmem,
        scratch_shapes=[
            pltpu.VMEM((3, TILE), i32),
            pltpu.VMEM((3, TILE), i32),
            pltpu.VMEM((BLOCKS, TILE), i32),
            pltpu.VMEM((SLOTS, TILE, TILE), bf16),
            pltpu.VMEM((SLOTS, TILE, TILE), bf16),
            pltpu.VMEM((ROWS, NODES * TILE), bf16),
            pltpu.VMEM((TERMS, HALVES, 2, BLOCKS, WIDTH, TILE), bf16),
            pltpu.VMEM((2, BLOCKS, WIDTH, TILE), bf16),
            pltpu.VMEM((TERMS, HALVES, 2, len(READERS[2]), WIDTH, TILE), bf16),
            pltpu.VMEM((TERMS, HALVES, NODES, WIDTH, TILE), bf16),
            pltpu.VMEM((TERMS, HALVES, len(DIRECT) + 1, WIDTH, TILE), bf16),
            pltpu.VMEM((TERMS, HALVES, BLOCKS, WIDTH, TILE), bf16),
            pltpu.VMEM((TERMS, width, ROWS), f32),
            pltpu.VMEM((TERMS, COLS, 1, ROWS), f32),
            pltpu.VMEM((width, ROWS), i32),
            pltpu.VMEM((8, TILE), i32),
            pltpu.SMEM((8, TILE), i32),
            pltpu.VMEM((KNOWN, 1, TILE), i32),
            pltpu.SMEM((KNOWN, 1, TILE), i32),
            pltpu.SemaphoreType.DMA((CHUNKS,)),
            pltpu.SemaphoreType.DMA((8,)),
            pltpu.SemaphoreType.DMA,
            pltpu.SemaphoreType.DMA,
            pltpu.SemaphoreType.DMA((TERMS, HALVES, 2)),
            pltpu.SemaphoreType.DMA((TERMS, HALVES, 2)),
            pltpu.SemaphoreType.DMA((TERMS, HALVES)),
            pltpu.SemaphoreType.DMA((TERMS, HALVES, len(GROUPS))),
            pltpu.SemaphoreType.DMA((TERMS,)),
            pltpu.SemaphoreType.DMA((TERMS,)),
        ],
        compiler_params=pltpu.CompilerParams(
            collective_id=0, has_side_effects=True, vmem_limit_bytes=60 << 20
        ),
        cost_estimate=pl.CostEstimate(
            flops=2 * TERMS * width * ROWS * NODES * TILE,
            bytes_accessed=SLOTS * TILE * TILE * 2,
            transcendentals=0,
        ),
        name="embed",
    )(
        tile_rows.reshape(3, TILE),
        tile_cols.reshape(3, TILE),
        tile_live,
        degrees.reshape(BLOCKS, TILE),
        term_weights,
        projection.T,
        tile_values,
    )
    return out.T


def solution(mesh):
    placed = (
        P("node", None, None),
        P("node"),
        P("node"),
        P("node"),
        P("node"),
        P("node", "col"),
        P(),
    )
    return jax.shard_map(
        local, mesh=mesh, in_specs=placed, out_specs=P("node", "col"), check_vma=False
    )
```

time: 77 us -> 65.2 us (0.85)
  Pallas kernels: 71.7 us -> 62.8 us
  local copies, waits for them, and re-layouts: 4.38 us -> 1.57 us
    pallas_call x1, Pallas kernels: 71.7 us -> 62.8 us  [local(): pl.pallas_call(kernel, out_shape=jax.ShapeDtypeStruct((width, ROWS), f32)...]
    unnamed x10 -> x1, local copies, waits for them, and re-layouts: 4.38 us -> 1.57 us
where the time goes in v2:
time: 65.2 us; the launch traced here: 65.1 us
  Pallas kernels  62.8 us (96%)
  local copies, waits for them, and re-layouts  1.57 us (2%)
  between operations  0.66 us (1%)
    pallas_call x1, Pallas kernels, local(): pl.pallas_call(kernel, out_shape=jax.ShapeDtypeStruct((width, ROWS), f32)...  62.8 us
    unnamed x1, local copies, waits for them, and re-layouts  1.57 us

profile of v2, /device:TPU:1, one launch (start us, length us, event | category | flops | bytes accessed | tf_op | source)
XLA Modules:
  0.0 65.1 jit_solution(8696082852295406799)
XLA Ops:
  0.7 62.8 %embed.1 = f32[64,512]{1,0:T(8,128)} custom-call(s32[3,128]{1,0:T(4,128)} %bitcast.7, s32[3,128]{1,0:T(4,128)} %bitcast.8, s32[1]{0:T(128)S(6)} %copy.9.live_ref, s32[4,128]{1,0:T(4,128)} %bitcast.9, f32[4]{0:T(128)} %weights_ref.1, s32[64,512]{1,0:T(8,128)} %bitcast.6, bf16[384,128,128]{2,1,0:T(8,128)(2,1)} %values_hbm.1), custom_call_target="tpu_custom_call" | custom-call | flops 1073741824 | bytes 12582912 | tf_op jit(solution)/shard_map/embed/pallas_call | solution.py:354
  63.5 1.6 %copy.10 = f32[512,64]{0,1:T(8,128)} copy(f32[512,64]{0,1:T(8,128)} %bitcast.5) | data formatting | bytes 262144

commit v3 on v2

--- a/solution.py
+++ b/solution.py
@@ -271,15 +271,15 @@
         for r in range(BLOCKS):
             pair = r * NODES + s
             block = sums[meta[6, pair]] * meta[7, pair].astype(jnp.bfloat16)
-            matrix[r * TILE : (r + 1) * TILE, pl.ds(pl.multiple_of(s * TILE, TILE), TILE)] = block
+            matrix[pl.ds(pl.multiple_of(s * TILE, TILE), TILE), r * TILE : (r + 1) * TILE] = jnp.transpose(block)
         return 0
 
     lax.fori_loop(0, NODES, place_block, 0)
 
     def times(x, first, count):
-        part = matrix[:, first * TILE : (first + count) * TILE]
+        part = matrix[first * TILE : (first + count) * TILE, :]
         return lax.dot_general(
-            x, part, (((1,), (1,)), ((), ())), preferred_element_type=jnp.float32
+            x, part, (((1,), (0,)), ((), ())), preferred_element_type=jnp.float32
         )
 
     def square_copies(k):
@@ -362,7 +362,7 @@
             pltpu.VMEM((BLOCKS, TILE), i32),
             pltpu.VMEM((SLOTS, TILE, TILE), bf16),
             pltpu.VMEM((SLOTS, TILE, TILE), bf16),
-            pltpu.VMEM((ROWS, NODES * TILE), bf16),
+            pltpu.VMEM((NODES * TILE, ROWS), bf16),
             pltpu.VMEM((TERMS, HALVES, 2, BLOCKS, WIDTH, TILE), bf16),
             pltpu.VMEM((2, BLOCKS, WIDTH, TILE), bf16),
             pltpu.VMEM((TERMS, HALVES, 2, len(READERS[2]), WIDTH, TILE), bf16),

time: 65.2 us -> 64.5 us (0.989)
    pallas_call x1, Pallas kernels: 62.8 us -> 62.2 us  [local(): pl.pallas_call(kernel, out_shape=jax.ShapeDtypeStruct((width, ROWS), f32)...]
where the time goes in v3:
time: 64.5 us; the launch traced here: 64.4 us
  Pallas kernels  62.2 us (96%)
  local copies, waits for them, and re-layouts  1.57 us (2%)
  between operations  0.66 us (1%)
    pallas_call x1, Pallas kernels, local(): pl.pallas_call(kernel, out_shape=jax.ShapeDtypeStruct((width, ROWS), f32)...  62.2 us
    unnamed x1, local copies, waits for them, and re-layouts  1.57 us

profile of v3, /device:TPU:1, one launch (start us, length us, event | category | flops | bytes accessed | tf_op | source)
XLA Modules:
  0.0 64.4 jit_solution(15232705399132267997)
XLA Ops:
  0.7 62.2 %embed.1 = f32[64,512]{1,0:T(8,128)} custom-call(s32[3,128]{1,0:T(4,128)} %bitcast.7, s32[3,128]{1,0:T(4,128)} %bitcast.8, s32[1]{0:T(128)S(6)} %copy.9.live_ref, s32[4,128]{1,0:T(4,128)} %bitcast.9, f32[4]{0:T(128)} %weights_ref.1, s32[64,512]{1,0:T(8,128)} %bitcast.6, bf16[384,128,128]{2,1,0:T(8,128)(2,1)} %values_hbm.1), custom_call_target="tpu_custom_call" | custom-call | flops 1073741824 | bytes 12582912 | tf_op jit(solution)/shard_map/embed/pallas_call | solution.py:354
  62.8 1.6 %copy.10 = f32[512,64]{0,1:T(8,128)} copy(f32[512,64]{0,1:T(8,128)} %bitcast.5) | data formatting | bytes 262144
